TPU v7x, 128 devices: a whole 4x4x4 slice. The times are simulated.
128 devices in a mesh: narrow: 4 (over z_hi, core), wide: 32 (over x, z_lo, y).
Axes of the slice: x: 4, y: 4, z: 4 (z_hi: 2, z_lo: 2; z = z_hi * 2 + z_lo), core: 2. Of those that a mesh axis runs over, the one named last changes fastest.
Arguments:
- panel: float32 [524288, 128], P(('narrow', 'wide')), may hold values from -6 to 6
- flips: int32 [524288], P(('narrow', 'wide')), may hold values from 0 to 1
- picks: int32 [8192], replicated, may hold values from 0 to 524287, as said below
Outputs:
- mixed: float32 [524288, 128], P(('narrow', 'wide'))
- sketch: float32 [8192, 128], P(('narrow', 'wide'))
- gram: float32 [128, 128], replicated
Inputs may be any that keep to these rules, and one draw needn't show every extreme that they name: Split picks into aligned blocks of 64 entries, one block for each device in the order of narrow+wide. In every block, at most 1 entries name rows of any one device's block of 4096 rows, and some device's block is named exactly 1 times. Within a device's block the row is uniform; repeats may occur.
All inputs are finite; a program needn't handle non-finite values.
Results may differ from a plain program's by a relative error of at most 0.00011.
Values sent between devices are 32-bit elements; how exact they have to be, the bound alone decides.
A program may use at most 64 MiB of HBM per device.

v0:
```python
import jax
import jax.numpy as jnp
from jax import lax
from jax.sharding import PartitionSpec as P


def from_partner(value, axis, apart):
    mask = 2**apart
    pairs = [(source, source ^ mask) for source in range(lax.axis_size(axis))]
    return lax.ppermute(value, axis, pairs)


def hadamard(order):
    index = jnp.arange(order, dtype=jnp.int32)
    both = index[:, None] & index[None, :]
    parity = jnp.zeros((order, order), jnp.int32)
    level = 0
    while 1 << level < order:
        parity = parity ^ both >> level & 1
        level += 1
    return (1 - 2 * parity).astype(jnp.float32)


def on_device(panel, flips, picks):
    rows_here, width = panel.shape
    inner = rows_here // 64
    devices = lax.axis_size("narrow") * lax.axis_size("wide")
    signed = panel * (1 - 2 * flips).astype(jnp.float32)[:, None]
    shaped = signed.reshape(64, inner, width)
    shaped = jnp.einsum("ap,pqc->aqc", hadamard(64), shaped, precision=lax.Precision.HIGHEST)
    shaped = jnp.einsum("bq,aqc->abc", hadamard(inner), shaped, precision=lax.Precision.HIGHEST)
    local = shaped.reshape(rows_here, width)
    for level in range(lax.axis_size("narrow").bit_length() - 1):
        partner = from_partner(local, "narrow", level)
        upper = lax.axis_index("narrow") >> level & 1 == 1
        local = jnp.where(upper, partner - local, local + partner)
    for level in range(lax.axis_size("wide").bit_length() - 1):
        partner = from_partner(local, "wide", level)
        upper = lax.axis_index("wide") >> level & 1 == 1
        local = jnp.where(upper, partner - local, local + partner)
    mixed = local * (1.0 / float(rows_here * devices) ** 0.5)
    me = lax.axis_index(("narrow", "wide"))
    base = me * rows_here
    wanted = picks - base
    owned = (wanted >= 0) & (wanted < rows_here)
    chosen = jnp.take(mixed, jnp.clip(wanted, 0, rows_here - 1), axis=0)
    sketch = lax.psum_scatter(
        jnp.where(owned[:, None], chosen, jnp.zeros_like(chosen)),
        ("narrow", "wide"),
        scatter_dimension=0,
        tiled=True,
    )
    total = float(picks.shape[0])
    part = jnp.dot(
        sketch.T, sketch, precision=lax.Precision.HIGHEST, preferred_element_type=jnp.float32
    )
    gram = lax.psum(part, ("narrow", "wide")) / total
    return (mixed, sketch, gram)


def solution(mesh):
    in_specs = (P(("narrow", "wide"), None), P(("narrow", "wide")), P())
    out_specs = (P(("narrow", "wide"), None), P(("narrow", "wide"), None), P())
    return jax.shard_map(
        on_device, mesh=mesh, in_specs=in_specs, out_specs=out_specs, check_vma=False
    )
```

profile of v0, /device:TPU:1, one launch (start us, length us, event | category | flops | bytes accessed | tf_op | source)
XLA Modules:
  0.0 1147.9 jit_solution(18260874863490580994)
XLA Ops:
  7.9 2.2 broadcast_multiply_fusion
  10.1 3.0 fusion.2
  13.2 3.3 fusion
  18.0 3.9 collective-permute-done
  21.9 2.4 add_select_fusion.5
  24.3 3.8 collective-permute-start.1
  28.1 45.8 %collective-permute-done.1 = f32[4096,128]{1,0:T(8,128)} collective-permute-done((f32[4096,128]{1,0:T(8,128)S(1)}, f32[4096,128]{1,0:T(8,128)}, u32[]{:S(2)}, u32[]{:S(2)}) %collective-permute-start.1) | collective-permute-done | bytes 2097184 | tf_op jit(solution)/shard_map/ppermute | solution.py:10
  73.9 2.4 add_select_fusion.4
  77.7 45.1 %collective-permute-done.2 = f32[4096,128]{1,0:T(8,128)} collective-permute-done((f32[4096,128]{1,0:T(8,128)S(1)}, f32[4096,128]{1,0:T(8,128)}, u32[]{:S(2)}, u32[]{:S(2)}) %collective-permute-start.2) | collective-permute-done | bytes 2097184 | tf_op jit(solution)/shard_map/ppermute | solution.py:10
  122.8 3.1 add_select_fusion.3
  125.9 2.9 collective-permute-start.3
  128.9 44.2 %collective-permute-done.3 = f32[4096,128]{1,0:T(8,128)} collective-permute-done((f32[4096,128]{1,0:T(8,128)}, f32[4096,128]{1,0:T(8,128)}, u32[]{:S(2)}, u32[]{:S(2)}) %collective-permute-start.3) | collective-permute-done | bytes 2097184 | tf_op jit(solution)/shard_map/ppermute | solution.py:10
  173.1 2.4 add_select_fusion.2
  175.6 44.5 %collective-permute-done.4 = f32[4096,128]{1,0:T(8,128)} collective-permute-done((f32[4096,128]{1,0:T(8,128)S(1)}, f32[4096,128]{1,0:T(8,128)}, u32[]{:S(2)}, u32[]{:S(2)}) %collective-permute-start.4) | collective-permute-done | bytes 2097184 | tf_op jit(solution)/shard_map/ppermute | solution.py:10
  220.1 3.1 add_select_fusion.1
  224.5 42.6 %collective-permute-done.5 = f32[4096,128]{1,0:T(8,128)} collective-permute-done((f32[4096,128]{1,0:T(8,128)}, f32[4096,128]{1,0:T(8,128)}, u32[]{:S(2)}, u32[]{:S(2)}) %collective-permute-start.5) | collective-permute-done | bytes 2097184 | tf_op jit(solution)/shard_map/ppermute | solution.py:10
  267.1 2.4 add_select_fusion
  269.5 2.8 collective-permute-start.6
  272.4 41.4 %collective-permute-done.6 = f32[4096,128]{1,0:T(8,128)} collective-permute-done((f32[4096,128]{1,0:T(8,128)S(1)}, f32[4096,128]{1,0:T(8,128)}, u32[]{:S(2)}, u32[]{:S(2)}) %collective-permute-start.6) | collective-permute-done | bytes 2097184 | tf_op jit(solution)/shard_map/ppermute | solution.py:10
  313.8 2.5 select_multiply_fusion
  316.3 27.7 %gather_fusion = f32[8192,128]{1,0:T(8,128)} fusion(f32[4096,128]{1,0:T(8,128)S(1)} %select_multiply_fusion, s32[8192]{0:T(1024)S(1)} %fusion.8), kind=kCustom, calls=%fused_computation | custom fusion | bytes 8421376 | tf_op jit(solution)/shard_map/jit(_take)/gather | solution.py:46
  344.1 7.6 select_select_fusion
  351.8 587.5 %reduce-scatter.2.cloned.1.call-done = f32[64,128]{1,0:T(8,128)} async-done(((f32[8192,128]{1,0:T(8,128)}), f32[64,128]{1,0:T(8,128)}) %reduce-scatter.2.cloned.1.call-update) | async-done | bytes 32784 | tf_op jit(solution)/shard_map/reduce_scatter | solution.py:47
  941.0 198.5 %all-reduce.2.cloned.1.call-done = f32[128,128]{1,0:T(8,128)} async-done(((f32[128,128]{1,0:T(8,128)}), f32[128,128]{1,0:T(8,128)}) %all-reduce.2.cloned.1.call-update) | async-done | bytes 65552 | tf_op jit(solution)/shard_map/psum | solution.py:57
  (23 shorter events, 8.3 us)
Async XLA Ops:
  7.2 932.1 %reduce-scatter.2.cloned.1.call-start = ((), (), s32[]{:S(2)}) async-start(), calls=%async_computation.1 | async-start | bytes 4227072 | tf_op jit(solution)/shard_map/reduce_scatter | solution.py:47
  16.5 1.5 copy-start.3
  16.5 5.4 collective-permute-start
  24.3 3.8 copy-start.2
  24.3 49.6 %collective-permute-start.1 = (f32[4096,128]{1,0:T(8,128)S(1)}, f32[4096,128]{1,0:T(8,128)}, u32[]{:S(2)}, u32[]{:S(2)}) collective-permute-start(f32[4096,128]{1,0:T(8,128)S(1)} %add_select_fusion.5), channel_id=1, source_target_pairs={{0,64},{32,96},{64,0},{96,32},{1,65},{33,97},{65,1},{97,33},{2,66}... | collective-permute-start | bytes 6291464 | tf_op jit(solution)/shard_map/ppermute | solution.py:10
  76.4 46.4 %collective-permute-start.2 = (f32[4096,128]{1,0:T(8,128)S(1)}, f32[4096,128]{1,0:T(8,128)}, u32[]{:S(2)}, u32[]{:S(2)}) collective-permute-start(f32[4096,128]{1,0:T(8,128)S(1)} %add_select_fusion.4), channel_id=1, source_target_pairs={{0,1},{1,0},{2,3},{3,2},{4,5},{5,4},{6,7},{7,6},{8,9},{9,8},{10,11... | collective-permute-start | bytes 6291464 | tf_op jit(solution)/shard_map/ppermute | solution.py:10
  125.9 47.2 %collective-permute-start.3 = (f32[4096,128]{1,0:T(8,128)}, f32[4096,128]{1,0:T(8,128)}, u32[]{:S(2)}, u32[]{:S(2)}) collective-permute-start(f32[4096,128]{1,0:T(8,128)} %add_select_fusion.3), channel_id=1, source_target_pairs={{0,2},{1,3},{2,0},{3,1},{4,6},{5,7},{6,4},{7,5},{8,10},{9,11},{10,... | collective-permute-start | bytes 6291464 | tf_op jit(solution)/shard_map/ppermute | solution.py:10
  175.5 44.6 %collective-permute-start.4 = (f32[4096,128]{1,0:T(8,128)S(1)}, f32[4096,128]{1,0:T(8,128)}, u32[]{:S(2)}, u32[]{:S(2)}) collective-permute-start(f32[4096,128]{1,0:T(8,128)S(1)} %add_select_fusion.2), channel_id=1, source_target_pairs={{0,4},{1,5},{2,6},{3,7},{4,0},{5,1},{6,2},{7,3},{8,12},{9,13},{10,... | collective-permute-start | bytes 6291464 | tf_op jit(solution)/shard_map/ppermute | solution.py:10
  223.3 43.8 %collective-permute-start.5 = (f32[4096,128]{1,0:T(8,128)}, f32[4096,128]{1,0:T(8,128)}, u32[]{:S(2)}, u32[]{:S(2)}) collective-permute-start(f32[4096,128]{1,0:T(8,128)} %add_select_fusion.1), channel_id=1, source_target_pairs={{0,8},{1,9},{2,10},{3,11},{4,12},{5,13},{6,14},{7,15},{8,0},{9,1},... | collective-permute-start | bytes 6291464 | tf_op jit(solution)/shard_map/ppermute | solution.py:10
  224.5 47.9 %copy-start.4 = (s32[8192]{0:T(1024)S(1)}, s32[8192]{0:T(1024)}, u32[]{:S(2)}) copy-start(s32[8192]{0:T(1024)} %param.5) | copy-start | bytes 98308
  269.5 2.9 copy-start.1
  269.5 44.3 %collective-permute-start.6 = (f32[4096,128]{1,0:T(8,128)S(1)}, f32[4096,128]{1,0:T(8,128)}, u32[]{:S(2)}, u32[]{:S(2)}) collective-permute-start(f32[4096,128]{1,0:T(8,128)S(1)} %add_select_fusion), channel_id=1, source_target_pairs={{0,16},{1,17},{2,18},{3,19},{4,20},{5,21},{6,22},{7,23},{8,24},{9,... | collective-permute-start | bytes 6291464 | tf_op jit(solution)/shard_map/ppermute | solution.py:10
  316.3 27.8 %copy-start = (f32[4096,128]{1,0:T(8,128)}, f32[4096,128]{1,0:T(8,128)S(1)}, u32[]{:S(2)}) copy-start(f32[4096,128]{1,0:T(8,128)S(1)} %select_multiply_fusion) | copy-start | bytes 6291460
  351.7 787.9 %all-reduce.2.cloned.1.call-start = ((), (), s32[]{:S(2)}) async-start(), calls=%async_computation.2 | async-start | bytes 131072 | tf_op jit(solution)/shard_map/psum | solution.py:57
Sparse Core Ops, SparseCore 0:
  351.8 587.3 reduce-scatter.1
  945.3 194.2 all-reduce.1
where the time goes:
time: 1150 us
  waiting for transfers between devices  1050 us (91%)
  other arithmetic  30.6 us (3%)
  local copies, waits for them, and re-layouts  27.8 us (2%)
  between operations  14.2 us (1%)
  starting transfers between devices  13.7 us (1%)
    reduce_scatter x1, waiting for transfers between devices, on_device(): lax.psum_scatter(jnp.where(owned[:, None], chosen, jnp.zeros_like(chosen)...  588 us
    ppermute x7, waiting for transfers between devices, from_partner(): return lax.ppermute(value, axis, pairs)  268 us
    psum x1, waiting for transfers between devices, on_device(): gram = lax.psum(part, ('narrow', 'wide')) / total  199 us
    gather x1, local copies, waits for them, and re-layouts, on_device(): chosen = jnp.take(mixed, jnp.clip(wanted, 0, rows_here - 1), axis=0)  27.7 us
  transfers between devices with their start and end apart: 9, of which 9 were waited for; matrix products, arithmetic and copies ran while one was open for 0% of the time, Pallas kernels for 0%

commit v1 on v0

v1 whole, which is shorter than its diff:
```python
import functools

import jax
import jax.numpy as jnp
from jax import lax
from jax.experimental import pallas as pl
from jax.experimental.pallas import tpu as pltpu
from jax.sharding import PartitionSpec as P

MESH = pl.DeviceIdType.MESH
DEV = 128
ROWS = 4096
COLS = 128
CHUNK = 32
HALF = 16
SCALE = 1.0 / float(ROWS * DEV) ** 0.5


def place(flat):
    return (flat // 32, flat % 32)


def partner(me, k):
    off = (k * 37) & 127
    y = (me + off) & 3
    z = (((me >> 2) & 1) + ((me >> 5) & 2) + (off >> 2)) & 3
    x = ((me >> 3) + (off >> 4)) & 3
    core = ((me >> 5) ^ (off >> 6)) & 1
    return y + (z & 1) * 4 + x * 8 + core * 32 + (z >> 1) * 64


def each_partner(me, body):
    def step(k, carry):
        body(partner(me, k))
        return carry

    lax.fori_loop(1, DEV, step, 0)


def butterfly(values):
    values = list(values)
    apart = 1
    while apart < len(values):
        for i in range(len(values)):
            if i & apart == 0:
                a, b = values[i], values[i + apart]
                values[i], values[i + apart] = a + b, a - b
        apart *= 2
    return values


def local_transform(x_ref, signs_ref, t_ref):
    def first(g, carry):
        base = pl.multiple_of(g * 128, 128)
        pick = (lax.broadcasted_iota(jnp.int32, (32, COLS), 0) == g).astype(jnp.float32)
        sign = jnp.dot(signs_ref[...], pick, preferred_element_type=jnp.float32)
        rows = x_ref[pl.ds(base, 128), :] * sign
        out = butterfly([rows[8 * m : 8 * m + 8] for m in range(16)])
        for m in range(16):
            t_ref[pl.ds(base + 8 * m, 8), :] = out[m]
        return carry

    lax.fori_loop(0, 32, first, 0)

    def second(g, carry):
        base = (g // 2) * 256 + (g % 2) * 64
        spots = [base + 128 * h + k for h in range(2) for k in range(8)]
        out = butterfly([t_ref[pl.ds(s, 8, stride=8), :] for s in spots])
        for s, value in zip(spots, out):
            t_ref[pl.ds(s, 8, stride=8), :] = value
        return carry

    lax.fori_loop(0, 32, second, 0)

    def third(g, carry):
        spots = [pl.multiple_of(g * 8 + 256 * m, 8) for m in range(16)]
        out = butterfly([t_ref[pl.ds(s, 8), :] for s in spots])
        for s, value in zip(spots, out):
            t_ref[pl.ds(s, 8), :] = value
        return carry

    lax.fori_loop(0, 32, third, 0)


def device_transform(half, src_ref, dst_ref):
    def low(g, carry):
        for u in range(2):
            rows = pl.ds(half * HALF + 8 * u, 8)
            out = butterfly([src_ref[g * 16 + m, rows, :] for m in range(16)])
            for m in range(16):
                dst_ref[g * 16 + m, rows, :] = out[m]
        return carry

    lax.fori_loop(0, 8, low, 0)

    def high(g, carry):
        for u in range(2):
            rows = pl.ds(half * HALF + 8 * u, 8)
            out = butterfly([dst_ref[g + 16 * m, rows, :] for m in range(8)])
            for m in range(8):
                dst_ref[g + 16 * m, rows, :] = out[m] * SCALE
        return carry

    lax.fori_loop(0, 16, high, 0)


def counts_of(me, picks_ref):
    def step(k, total):
        p = picks_ref[pl.ds(k, 1), :]
        here = ((p >> 5) & 127) == me
        q = (p >> 12) * CHUNK + (p & 31)
        hi = jnp.where(here, q >> 7, -1)
        lo = q & 127
        a = (lax.broadcasted_iota(jnp.int32, (32, 128), 0) == hi).astype(jnp.float32)
        b = (lax.broadcasted_iota(jnp.int32, (128, 128), 0) == lo).astype(jnp.float32)
        return total + lax.dot_general(
            a, b, (((1,), (1,)), ((), ())), preferred_element_type=jnp.float32
        )

    return lax.fori_loop(0, 64, step, jnp.zeros((32, 128), jnp.float32))


def kernel(
    panel_ref, flips_ref, picks_ref, picks_any,
    mixed_ref, sketch_ref, gram_ref,
    x_ref, t_ref, in_ref, done_ref, signs_ref, counts_ref, wanted_ref, wanted_sm, mine_sm,
    sk_out, sk_in, gp_out, gp_in, gs_out, gs_in,
    load_sem, small_sem, own_sem, p1s, p1r, p2s, p2r, sks, skr, gps, gpr, gss, gsr,
):
    me = lax.axis_index("narrow") * 32 + lax.axis_index("wide")
    load = pltpu.make_async_copy(panel_ref, x_ref, load_sem)
    load.start()
    mine = pltpu.make_async_copy(picks_any.at[me // 2], mine_sm, small_sem.at[0])
    mine.start()

    barrier = pltpu.get_barrier_semaphore()
    each_partner(
        me,
        lambda d: pl.semaphore_signal(barrier, inc=1, device_id=place(d), device_id_type=MESH),
    )

    p = picks_ref[...]
    lane = lax.broadcasted_iota(jnp.int32, p.shape, 1)
    local = jnp.where((p >> 12) == me, p & (ROWS - 1), 0)
    even = jnp.max(jnp.where(lane < 64, local, 0), axis=1, keepdims=True)
    odd = jnp.max(jnp.where(lane < 64, 0, local), axis=1, keepdims=True)
    wanted_ref[...] = jnp.where(lane == 0, even, odd)
    wanted = pltpu.make_async_copy(wanted_ref, wanted_sm, small_sem.at[1])
    wanted.start()

    signs_ref[...] = (1 - 2 * flips_ref[...]).astype(jnp.float32).T
    load.wait()
    local_transform(x_ref, signs_ref, t_ref)
    pl.semaphore_wait(barrier, DEV - 1)

    def rows_of(d, half):
        return pl.ds(pl.multiple_of(d * CHUNK + half * HALF, HALF), HALF)

    def send_in(half):
        def one(d):
            pltpu.make_async_remote_copy(
                t_ref.at[rows_of(d, half)], in_ref.at[me, pl.ds(half * HALF, HALF)],
                p1s.at[half], p1r.at[half], device_id=place(d), device_id_type=MESH,
            ).start()

        each_partner(me, one)

    def send_back(half):
        def one(d):
            pltpu.make_async_remote_copy(
                done_ref.at[d, pl.ds(half * HALF, HALF)], mixed_ref.at[rows_of(me, half)],
                p2s.at[half], p2r.at[half], device_id=place(d), device_id_type=MESH,
            ).start()

        each_partner(me, one)

    others = pl.ds(0, (DEV - 1) * HALF)

    def wait_bytes(sem):
        pltpu.make_async_copy(x_ref.at[others], t_ref.at[others], sem).wait()

    send_in(0)
    send_in(1)
    in_ref[me] = t_ref[pl.ds(pl.multiple_of(me * CHUNK, CHUNK), CHUNK), :]
    counts_ref[...] = counts_of(me, picks_ref)

    wait_bytes(p1r.at[0])
    device_transform(0, in_ref, done_ref)
    send_back(0)
    wait_bytes(p1r.at[1])
    device_transform(1, in_ref, done_ref)
    mixed_ref[pl.ds(pl.multiple_of(me * CHUNK, CHUNK), CHUNK), :] = done_ref[me]

    def gram_step(g, total):
        rows = done_ref[pl.ds(g * 4, 4)].reshape(128, COLS)
        left = rows.T * counts_ref[pl.ds(g, 1), :]
        return total + jnp.dot(
            left, rows, precision=lax.Precision.HIGHEST, preferred_element_type=jnp.float32
        )

    part = lax.fori_loop(0, 32, gram_step, jnp.zeros((COLS, COLS), jnp.float32))
    gp_out[...] = part.reshape(COLS, 1, COLS)

    def row_to(src, dst, send, recv, d):
        pltpu.make_async_remote_copy(
            src, dst, send, recv, device_id=place(d), device_id_type=MESH
        ).start()

    def wait_rows(sem):
        pltpu.make_async_copy(
            sk_out.at[pl.ds(0, DEV - 1)], sk_in.at[pl.ds(0, DEV - 1)], sem
        ).wait()

    each_partner(me, lambda d: row_to(gp_out.at[d], gp_in.at[me], gps, gpr, d))
    gp_in[me] = gp_out[me]
    send_back(1)

    wait_rows(gpr)
    gs_out[...] = jnp.sum(gp_in[...], axis=0, keepdims=True) * (1.0 / 8192.0)
    each_partner(me, lambda d: row_to(gs_out.at[0], gs_in.at[me], gss, gsr, d))
    gs_in[me] = gs_out[0]

    wait_bytes(p2r.at[0])
    wait_bytes(p2r.at[1])
    wanted.wait()

    def row_for(d):
        sk_out[d] = mixed_ref[pl.ds(wanted_sm[d // 2, d % 2], 1), :]

    def send_row(d):
        row_for(d)
        row_to(sk_out.at[d], sk_in.at[me], sks, skr, d)

    each_partner(me, send_row)
    row_for(me)
    sk_in[me] = sk_out[me]

    wait_rows(gsr)
    gram_ref[...] = gs_in[...].reshape(COLS, COLS)
    mine.wait()
    wait_rows(skr)
    start = (me % 2) * 64

    def pick_row(i, carry):
        owner = (mine_sm[start + i] >> 12) & (DEV - 1)
        sketch_ref[pl.ds(i, 1), :] = sk_in[owner]
        return carry

    lax.fori_loop(0, 64, pick_row, 0)
    for half in range(2):
        wait_bytes(p1s.at[half])
        wait_bytes(p2s.at[half])
    wait_rows(gps)
    wait_rows(gss)
    wait_rows(sks)


def on_device(panel, flips, picks):
    vmem = pl.BlockSpec(memory_space=pltpu.VMEM)
    hbm = pl.BlockSpec(memory_space=pl.ANY)
    dma = pltpu.SemaphoreType.DMA
    f32 = jnp.float32
    row = pltpu.VMEM((DEV, 1, COLS), f32)
    picks = picks.reshape(64, 128)
    return pl.pallas_call(
        kernel,
        out_shape=(
            jax.ShapeDtypeStruct((ROWS, COLS), f32),
            jax.ShapeDtypeStruct((64, COLS), f32),
            jax.ShapeDtypeStruct((COLS, COLS), f32),
        ),
        in_specs=[hbm, vmem, vmem, hbm],
        out_specs=(vmem, vmem, vmem),
        scratch_shapes=[
            pltpu.VMEM((ROWS, COLS), f32),
            pltpu.VMEM((ROWS, COLS), f32),
            pltpu.VMEM((DEV, CHUNK, COLS), f32),
            pltpu.VMEM((DEV, CHUNK, COLS), f32),
            pltpu.VMEM((128, 32), f32),
            pltpu.VMEM((32, 128), f32),
            pltpu.VMEM((64, 128), jnp.int32),
            pltpu.SMEM((64, 128), jnp.int32),
            pltpu.SMEM((128,), jnp.int32),
            row, row, row, row, pltpu.VMEM((1, 1, COLS), f32), row,
            dma, dma((2,)), dma, dma((2,)), dma((2,)), dma((2,)), dma((2,)),
            dma, dma, dma, dma, dma, dma,
        ],
        name="sketch",
        compiler_params=pltpu.CompilerParams(
            collective_id=1, has_side_effects=True, vmem_limit_bytes=40 * 2**20
        ),
    )(panel, flips.reshape(32, 128), picks, picks)


def solution(mesh):
    both = ("narrow", "wide")
    return jax.shard_map(
        on_device,
        mesh=mesh,
        in_specs=(P(both, None), P(both), P()),
        out_specs=(P(both, None), P(both, None), P()),
        check_vma=False,
    )
```

time: 1150 us -> 85.6 us (0.07)
  waiting for transfers between devices: 1050 us -> 0 us
  Pallas kernels: 0 us -> 79.1 us
  other arithmetic: 30.6 us -> 0 us
  local copies, waits for them, and re-layouts: 27.8 us -> 5.62 us
  starting transfers between devices: 13.7 us -> 0 us
  between operations: 14.2 us -> 0.65 us
    reduce_scatter x1 -> x0, waiting for transfers between devices: 588 us -> none  [on_device(): lax.psum_scatter(jnp.where(owned[:, None], chosen, jnp.zeros_like(chosen)...]
    ppermute x7 -> x0, waiting for transfers between devices: 268 us -> none  [from_partner(): return lax.ppermute(value, axis, pairs)]
    psum x1 -> x0, waiting for transfers between devices: 199 us -> none  [on_device(): gram = lax.psum(part, ('narrow', 'wide')) / total]
    pallas_call x0 -> x1, Pallas kernels: none -> 79.1 us  [on_device(): pl.pallas_call(kernel, out_shape=(jax.ShapeDtypeStruct((ROWS, COLS), f32)...]
    gather x1 -> x0, local copies, waits for them, and re-layouts: 27.7 us -> none  [on_device(): chosen = jnp.take(mixed, jnp.clip(wanted, 0, rows_here - 1), axis=0)]
    select_n x7 -> x0, other arithmetic: 23.6 us -> none  [the longest x6 16 us: on_device(): local = jnp.where(upper, partner - local, local + partner)]
    ppermute x7 -> x0, starting transfers between devices: 13.7 us -> none  [from_partner(): return lax.ppermute(value, axis, pairs)]
  transfers between devices with their start and end apart: 9 -> 0, of which waited for: 9 -> 0; matrix products, arithmetic and copies ran while one was open for 0% -> 0% of each run, Pallas kernels for 0% -> 0%
where the time goes in v1:
time: 85.6 us; the launch traced here: 85.3 us
  Pallas kernels  79.1 us (92%)
  local copies, waits for them, and re-layouts  5.62 us (7%)
    pallas_call x1, Pallas kernels, on_device(): pl.pallas_call(kernel, out_shape=(jax.ShapeDtypeStruct((ROWS, COLS), f32)...  79.1 us
    unnamed x9, local copies, waits for them, and re-layouts  5.62 us

profile of v1, /device:TPU:1, one launch (start us, length us, event | category | flops | bytes accessed | tf_op | source)
XLA Modules:
  0.0 85.3 jit_solution(17090612821532891801)
XLA Ops:
  0.6 0.0 copy-start
  0.6 1.6 %copy-done = f32[4096,128]{1,0:T(8,128)S(1)} copy-done((f32[4096,128]{1,0:T(8,128)S(1)}, f32[4096,128]{1,0:T(8,128)}, u32[]{:S(2)}) %copy-start) | copy-done | bytes 2097176
  2.2 0.0 copy-start.1
  2.2 0.8 copy-done.1
  3.0 0.0 copy-start.2
  3.0 0.7 copy-done.2
  3.7 79.1 %sketch.1 = (f32[4096,128]{1,0:T(8,128)S(1)}, f32[64,128]{1,0:T(8,128)S(1)}, f32[128,128]{1,0:T(8,128)S(1)}) custom-call(f32[4096,128]{1,0:T(8,128)S(1)} %copy-done, s32[32,128]{1,0:T(8,128)S(1)} %bitcast.4, s32[64,128]{1,0:T(8,128)S(1)} %bitcast.2, s32[64,128]{1,0:T(8,128)S(1)} %bitcast.3), custom_call_target="tpu_custom_call" | custom-call | tf_op jit(solution)/shard_map/sketch/pallas_call | solution.py:265
  82.8 1.3 %copy.9 = f32[4096,128]{1,0:T(8,128)} copy(f32[4096,128]{1,0:T(8,128)S(1)} %get-tuple-element.6) | data formatting | bytes 4194304
  84.1 0.6 copy.10
  84.7 0.6 copy.11
Async XLA Ops:
  0.6 1.6 %copy-start = (f32[4096,128]{1,0:T(8,128)S(1)}, f32[4096,128]{1,0:T(8,128)}, u32[]{:S(2)}) copy-start(f32[4096,128]{1,0:T(8,128)} %panel_ref.1) | copy-start | bytes 6291460
  2.2 0.8 copy-start.1
  3.0 0.7 copy-start.2

commit v2 on v1

v2 whole, which is shorter than its diff:
```python
import functools

import jax
import jax.numpy as jnp
from jax import lax
from jax.experimental import pallas as pl
from jax.experimental.pallas import tpu as pltpu
from jax.sharding import PartitionSpec as P

MESH = pl.DeviceIdType.MESH
DEV = 128
ROWS = 4096
COLS = 128
CHUNK = 32
HALF = 16
LOADS = 4
SCALE = 1.0 / float(ROWS * DEV) ** 0.5


def place(flat):
    return (flat // 32, flat % 32)


def partner(me, k):
    off = (k * 37) & 127
    y = (me + off) & 3
    z = (((me >> 2) & 1) + ((me >> 5) & 2) + (off >> 2)) & 3
    x = ((me >> 3) + (off >> 4)) & 3
    core = ((me >> 5) ^ (off >> 6)) & 1
    return y + (z & 1) * 4 + x * 8 + core * 32 + (z >> 1) * 64


def each_partner(me, body):
    def step(k, carry):
        body(partner(me, k))
        return carry

    lax.fori_loop(1, DEV, step, 0)


def butterfly(values):
    values = list(values)
    apart = 1
    while apart < len(values):
        for i in range(len(values)):
            if i & apart == 0:
                a, b = values[i], values[i + apart]
                values[i], values[i + apart] = a + b, a - b
        apart *= 2
    return values


def first_pass(x_ref, signs, t_ref, g):
    rows = x_ref[g * 128 : g * 128 + 128, :] * signs[:, g : g + 1]
    out = butterfly([rows[8 * m : 8 * m + 8] for m in range(16)])
    for m in range(16):
        t_ref[g * 128 + 8 * m : g * 128 + 8 * m + 8, :] = out[m]


def second_pass(t_ref):
    def step(g, carry):
        base = (g // 2) * 256 + (g % 2) * 64
        spots = [base + 128 * h + k for h in range(2) for k in range(8)]
        out = butterfly([t_ref[pl.ds(s, 8, stride=8), :] for s in spots])
        for s, value in zip(spots, out):
            t_ref[pl.ds(s, 8, stride=8), :] = value
        return carry

    lax.fori_loop(0, 32, step, 0, unroll=4)


def third_pass(half, t_ref):
    def step(g, carry):
        base = pl.multiple_of((g % 2) * 8 + half * HALF + (g // 2) * CHUNK, 8)
        spots = [base + 256 * m for m in range(16)]
        out = butterfly([t_ref[pl.ds(s, 8), :] for s in spots])
        for s, value in zip(spots, out):
            t_ref[pl.ds(s, 8), :] = value
        return carry

    lax.fori_loop(0, 16, step, 0, unroll=4)


def device_transform(half, src_ref, dst_ref):
    def low(g, carry):
        for u in range(2):
            rows = pl.ds(half * HALF + 8 * u, 8)
            out = butterfly([src_ref[g * 16 + m, rows, :] for m in range(16)])
            for m in range(16):
                dst_ref[g * 16 + m, rows, :] = out[m]
        return carry

    lax.fori_loop(0, 8, low, 0, unroll=2)

    def high(g, carry):
        for u in range(2):
            rows = pl.ds(half * HALF + 8 * u, 8)
            out = butterfly([dst_ref[g + 16 * m, rows, :] for m in range(8)])
            for m in range(8):
                dst_ref[g + 16 * m, rows, :] = out[m] * SCALE
        return carry

    lax.fori_loop(0, 16, high, 0, unroll=4)


def counts_of(me, picks_ref):
    def step(k, total):
        p = picks_ref[pl.ds(k, 1), :]
        here = ((p >> 5) & 127) == me
        q = ((p >> 4) & 1) * (DEV * HALF) + (p >> 12) * HALF + (p & 15)
        hi = jnp.where(here, q >> 7, -1)
        lo = q & 127
        a = (lax.broadcasted_iota(jnp.int32, (32, 128), 0) == hi).astype(jnp.float32)
        b = (lax.broadcasted_iota(jnp.int32, (128, 128), 0) == lo).astype(jnp.float32)
        return total + lax.dot_general(
            a, b, (((1,), (1,)), ((), ())), preferred_element_type=jnp.float32
        )

    return lax.fori_loop(0, 64, step, jnp.zeros((32, 128), jnp.float32))


def kernel(
    panel_ref, flips_hbm, picks_hbm,
    mixed_ref, sketch_ref, gram_ref,
    x_ref, t_ref, in_ref, done_ref, flips_ref, picks_ref, counts_ref, part_ref, wanted_ref, wanted_sm, mine_sm,
    row_out, row_in, gp_out, gp_in,
    load_sem, small_sem, p1s, p1r, p2s, p2r, rows_s, rows_r, gps, gpr,
):
    me = lax.axis_index("narrow") * 32 + lax.axis_index("wide")
    small = [
        pltpu.make_async_copy(flips_hbm, flips_ref, small_sem.at[0]),
        pltpu.make_async_copy(picks_hbm, picks_ref, small_sem.at[1]),
        pltpu.make_async_copy(picks_hbm.at[me // 2], mine_sm, small_sem.at[2]),
    ]
    for copy in small:
        copy.start()
    loads = []
    for i in range(LOADS):
        rows = pl.ds(i * (ROWS // LOADS), ROWS // LOADS)
        loads.append(pltpu.make_async_copy(panel_ref.at[rows], x_ref.at[rows], load_sem.at[i]))
        loads[-1].start()

    barrier = pltpu.get_barrier_semaphore()
    small[0].wait()
    signs = (1 - 2 * flips_ref[...]).astype(jnp.float32).T
    for g in range(32):
        for k in range(4 * g, 4 * g + 4):
            if k > 0:
                pl.semaphore_signal(
                    barrier, inc=1, device_id=place(partner(me, k)), device_id_type=MESH
                )
        if g % (32 // LOADS) == 0:
            loads[g // (32 // LOADS)].wait()
        first_pass(x_ref, signs, t_ref, g)
    second_pass(t_ref)
    third_pass(0, t_ref)
    pl.semaphore_wait(barrier, DEV - 1)

    def rows_of(d, half):
        return pl.ds(pl.multiple_of(d * CHUNK + half * HALF, HALF), HALF)

    def send_in(half):
        def one(d):
            pltpu.make_async_remote_copy(
                t_ref.at[rows_of(d, half)], in_ref.at[me, pl.ds(half * HALF, HALF)],
                p1s.at[half], p1r.at[half], device_id=place(d), device_id_type=MESH,
            ).start()

        each_partner(me, one)

    def send_back(half):
        def one(d):
            pltpu.make_async_remote_copy(
                done_ref.at[d, pl.ds(half * HALF, HALF)], mixed_ref.at[rows_of(me, half)],
                p2s.at[half], p2r.at[half], device_id=place(d), device_id_type=MESH,
            ).start()

        each_partner(me, one)

    others = pl.ds(0, (DEV - 1) * HALF)

    def wait_bytes(sem):
        pltpu.make_async_copy(x_ref.at[others], t_ref.at[others], sem).wait()

    def add_gram(half):
        def step(g, total):
            rows = done_ref[pl.ds(g * 8, 8), pl.ds(half * HALF, HALF), :].reshape(128, COLS)
            left = rows.T * counts_ref[pl.ds(half * 16 + g, 1), :]
            return total + jnp.dot(
                left, rows, precision=lax.Precision.HIGHEST, preferred_element_type=jnp.float32
            )

        part_ref[...] = lax.fori_loop(0, 16, step, part_ref[...])

    send_in(0)
    third_pass(1, t_ref)
    send_in(1)
    in_ref[me] = t_ref[pl.ds(pl.multiple_of(me * CHUNK, CHUNK), CHUNK), :]

    small[1].wait()
    p = picks_ref[...]
    lane = lax.broadcasted_iota(jnp.int32, p.shape, 1)
    local = jnp.where((p >> 12) == me, p & (ROWS - 1), 0)
    even = jnp.max(jnp.where(lane < 64, local, 0), axis=1, keepdims=True)
    odd = jnp.max(jnp.where(lane < 64, 0, local), axis=1, keepdims=True)
    wanted_ref[...] = jnp.where(lane == 0, even, odd)
    wanted = pltpu.make_async_copy(wanted_ref, wanted_sm, small_sem.at[1])
    wanted.start()
    counts_ref[...] = counts_of(me, picks_ref)
    part_ref[...] = jnp.zeros_like(part_ref)

    wait_bytes(p1r.at[0])
    device_transform(0, in_ref, done_ref)
    send_back(0)
    add_gram(0)
    wait_bytes(p1r.at[1])
    device_transform(1, in_ref, done_ref)
    send_back(1)
    mixed_ref[pl.ds(pl.multiple_of(me * CHUNK, CHUNK), CHUNK), :] = done_ref[me]
    add_gram(1)
    gp_out[...] = part_ref[...].reshape(COLS, 1, COLS)

    def send(src, dst, send_sem, recv_sem, d):
        pltpu.make_async_remote_copy(
            src, dst, send_sem, recv_sem, device_id=place(d), device_id_type=MESH
        ).start()

    def wait_rows(ref, sem):
        pltpu.make_async_copy(ref.at[pl.ds(0, DEV - 1)], ref.at[pl.ds(0, DEV - 1)], sem).wait()

    each_partner(me, lambda d: send(gp_out.at[d], gp_in.at[me], gps, gpr, d))
    gp_in[me] = gp_out[me]
    wait_rows(gp_in, gpr)
    gram_row = jnp.sum(gp_in[...], axis=0, keepdims=True) * (1.0 / 8192.0)
    row_out[:, 1:2, :] = jnp.broadcast_to(gram_row, (DEV, 1, COLS))

    wait_bytes(p2r.at[0])
    wait_bytes(p2r.at[1])
    wanted.wait()

    def row_for(d):
        row_out[d, 0:1, :] = mixed_ref[pl.ds(wanted_sm[d // 2, d % 2], 1), :]

    def send_row(d):
        row_for(d)
        send(row_out.at[d], row_in.at[me], rows_s, rows_r, d)

    each_partner(me, send_row)
    row_for(me)
    row_in[me] = row_out[me]

    small[2].wait()
    wait_rows(row_in, rows_r)
    gram_ref[...] = row_in[:, 1, :]
    start = (me % 2) * 64

    def pick_row(i, carry):
        owner = (mine_sm[start + i] >> 12) & (DEV - 1)
        sketch_ref[pl.ds(i, 1), :] = row_in[owner, 0:1, :]
        return carry

    lax.fori_loop(0, 64, pick_row, 0, unroll=8)
    for half in range(2):
        wait_bytes(p1s.at[half])
        wait_bytes(p2s.at[half])
    wait_rows(gp_in, gps)
    wait_rows(row_in, rows_s)


def leave_kernel(mixed_ref, sketch_ref, gram_ref, mixed_out, sketch_out, gram_out, sems):
    pairs = ((mixed_ref, mixed_out), (sketch_ref, sketch_out), (gram_ref, gram_out))
    copies = [pltpu.make_async_copy(a, b, sems.at[i]) for i, (a, b) in enumerate(pairs)]
    for copy in copies:
        copy.start()
    for copy in copies:
        copy.wait()


def on_device(panel, flips, picks):
    vmem = pl.BlockSpec(memory_space=pltpu.VMEM)
    hbm = pl.BlockSpec(memory_space=pltpu.HBM)
    dma = pltpu.SemaphoreType.DMA
    f32, i32 = jnp.float32, jnp.int32
    shapes = ((ROWS, COLS), (64, COLS), (COLS, COLS))
    parts = pl.pallas_call(
        kernel,
        out_shape=tuple(pltpu.VMEM(shape, f32) for shape in shapes),
        in_specs=[hbm, hbm, hbm],
        out_specs=(vmem, vmem, vmem),
        scratch_shapes=[
            pltpu.VMEM((ROWS, COLS), f32),
            pltpu.VMEM((ROWS, COLS), f32),
            pltpu.VMEM((DEV, CHUNK, COLS), f32),
            pltpu.VMEM((DEV, CHUNK, COLS), f32),
            pltpu.VMEM((32, 128), i32),
            pltpu.VMEM((64, 128), i32),
            pltpu.VMEM((32, 128), f32),
            pltpu.VMEM((COLS, COLS), f32),
            pltpu.VMEM((64, 128), i32),
            pltpu.SMEM((64, 128), i32),
            pltpu.SMEM((128,), i32),
            pltpu.VMEM((DEV, 2, COLS), f32),
            pltpu.VMEM((DEV, 2, COLS), f32),
            pltpu.VMEM((DEV, 1, COLS), f32),
            pltpu.VMEM((DEV, 1, COLS), f32),
            dma((LOADS,)), dma((3,)), dma((2,)), dma((2,)), dma((2,)), dma((2,)),
            dma, dma, dma, dma,
        ],
        name="sketch",
        compiler_params=pltpu.CompilerParams(
            collective_id=1, has_side_effects=True, vmem_limit_bytes=56 * 2**20
        ),
    )(panel, flips.reshape(32, 128), picks.reshape(64, 128))
    return pl.pallas_call(
        leave_kernel,
        out_shape=tuple(jax.ShapeDtypeStruct(shape, f32) for shape in shapes),
        in_specs=[vmem, vmem, vmem],
        out_specs=(hbm, hbm, hbm),
        scratch_shapes=[dma((3,))],
        name="leave",
    )(*parts)


def solution(mesh):
    both = ("narrow", "wide")
    return jax.shard_map(
        on_device,
        mesh=mesh,
        in_specs=(P(both, None), P(both), P()),
        out_specs=(P(both, None), P(both, None), P()),
        check_vma=False,
    )
```

time: 85.6 us -> 80.9 us (0.945)
  local copies, waits for them, and re-layouts: 5.62 us -> 2.54 us
  Pallas kernels: 79.1 us -> 77.5 us
    unnamed x9 -> x6, local copies, waits for them, and re-layouts: 5.62 us -> 2.54 us
    pallas_call x1 -> x2, Pallas kernels: 79.1 us -> 77.5 us  [the longest x1 74.6 us: on_device(): pl.pallas_call(kernel, out_shape=tuple((pltpu.VMEM(shape, f32) for shape...]
where the time goes in v2:
time: 80.9 us; the launch traced here: 80.7 us
  Pallas kernels  77.5 us (96%)
  local copies, waits for them, and re-layouts  2.54 us (3%)
    pallas_call x1, Pallas kernels, on_device(): pl.pallas_call(kernel, out_shape=tuple((pltpu.VMEM(shape, f32) for shape...  74.6 us
    pallas_call x1, Pallas kernels, on_device(): pl.pallas_call(leave_kernel, out_shape=tuple((jax.ShapeDtypeStruct(shape,...  2.97 us
    unnamed x6, local copies, waits for them, and re-layouts  2.54 us

profile of v2, /device:TPU:1, one launch (start us, length us, event | category | flops | bytes accessed | tf_op | source)
XLA Modules:
  0.0 80.7 jit_solution(17263694922089374204)
XLA Ops:
  0.6 74.6 %sketch.1 = (f32[4096,128]{1,0:T(8,128)S(1)}, f32[64,128]{1,0:T(8,128)S(1)}, f32[128,128]{1,0:T(8,128)S(1)}) custom-call(f32[4096,128]{1,0:T(8,128)} %panel_ref.1, s32[32,128]{1,0:T(8,128)} %bitcast.3, s32[64,128]{1,0:T(8,128)} %bitcast.2), custom_call_target="tpu_custom_call" | custom-call | tf_op jit(solution)/shard_map/sketch/pallas_call | solution.py:285
  75.2 0.0 copy-start
  75.2 1.3 %copy-done = f32[4096,128]{1,0:T(8,128)} copy-done((f32[4096,128]{1,0:T(8,128)}, f32[4096,128]{1,0:T(8,128)S(1)}, u32[]{:S(2)}) %copy-start) | copy-done | bytes 2097176
  76.5 0.0 copy-start.1
  76.5 0.6 copy-done.1
  77.1 0.0 copy-start.2
  77.1 0.6 copy-done.2
  77.7 3.0 %leave.1 = (f32[4096,128]{1,0:T(8,128)}, f32[64,128]{1,0:T(8,128)}, f32[128,128]{1,0:T(8,128)}) custom-call(f32[4096,128]{1,0:T(8,128)} %copy-done, f32[64,128]{1,0:T(8,128)} %copy-done.2, f32[128,128]{1,0:T(8,128)} %copy-done.1), custom_call_target="tpu_custom_call" | custom-call | tf_op jit(solution)/shard_map/leave/pallas_call | solution.py:314
Async XLA Ops:
  75.2 1.3 %copy-start = (f32[4096,128]{1,0:T(8,128)}, f32[4096,128]{1,0:T(8,128)S(1)}, u32[]{:S(2)}) copy-start(f32[4096,128]{1,0:T(8,128)S(1)} %get-tuple-element.6.mixed_ref) | copy-start | bytes 6291460
  76.5 0.6 copy-start.1
  77.1 0.6 copy-start.2

commit v3 on v2

--- a/solution.py
+++ b/solution.py
@@ -1,4 +1,4 @@
-import functools
+import itertools
 
 import jax
 import jax.numpy as jnp
@@ -17,25 +17,49 @@
 SCALE = 1.0 / float(ROWS * DEV) ** 0.5
 
 
-def place(flat):
-    return (flat // 32, flat % 32)
-
-
-def partner(me, k):
-    off = (k * 37) & 127
-    y = (me + off) & 3
-    z = (((me >> 2) & 1) + ((me >> 5) & 2) + (off >> 2)) & 3
-    x = ((me >> 3) + (off >> 4)) & 3
-    core = ((me >> 5) ^ (off >> 6)) & 1
-    return y + (z & 1) * 4 + x * 8 + core * 32 + (z >> 1) * 64
-
-
-def each_partner(me, body):
-    def step(k, carry):
-        body(partner(me, k))
-        return carry
-
-    lax.fori_loop(1, DEV, step, 0)
+def offsets():
+    rest = [o for o in itertools.product(range(4), range(4), range(4), range(2)) if any(o)]
+    used = [0] * 6
+    order = []
+
+    def load(o):
+        out = [0] * 6
+        for i in range(3):
+            out[2 * i] = (0, 1, 1, 0)[o[i]]
+            out[2 * i + 1] = (0, 0, 1, 1)[o[i]]
+        return out
+
+    def cost(o):
+        total = [u + w for u, w in zip(used, load(o))]
+        return -sum(load(o)), max(total) - min(total), max(total)
+
+    while rest:
+        best = min(rest, key=cost)
+        rest.remove(best)
+        order.append(best)
+        used = [u + w for u, w in zip(used, load(best))]
+    return order
+
+
+OFFSETS = offsets()
+
+
+class Place:
+    def __init__(self):
+        self.narrow, self.wide = lax.axis_index("narrow"), lax.axis_index("wide")
+        self.me = self.narrow * 32 + self.wide
+        y, z_lo, x = self.wide & 3, (self.wide >> 2) & 1, self.wide >> 3
+        core, z = self.narrow & 1, (self.narrow >> 1) * 2 + z_lo
+        self.xs = [((x + i) & 3) * 8 for i in range(4)]
+        self.ys = [(y + i) & 3 for i in range(4)]
+        self.zs = [((z + i) & 1) * 4 for i in range(4)]
+        self.zn = [(((z + i) >> 1) & 1) * 2 for i in range(4)]
+        self.cs = [core, 1 - core]
+
+    def others(self):
+        for dx, dy, dz, dc in OFFSETS:
+            narrow, wide = self.zn[dz] + self.cs[dc], self.xs[dx] + self.ys[dy] + self.zs[dz]
+            yield narrow * 32 + wide, (narrow, wide)
 
 
 def butterfly(values):
@@ -124,31 +148,30 @@
     mixed_ref, sketch_ref, gram_ref,
     x_ref, t_ref, in_ref, done_ref, flips_ref, picks_ref, counts_ref, part_ref, wanted_ref, wanted_sm, mine_sm,
     row_out, row_in, gp_out, gp_in,
-    load_sem, small_sem, p1s, p1r, p2s, p2r, rows_s, rows_r, gps, gpr,
+    load_sem, small_sem, p1s, p1r, p2s, p2r, gps, gpr, rows_s, rows_r,
 ):
-    me = lax.axis_index("narrow") * 32 + lax.axis_index("wide")
+    here = Place()
+    me = here.me
     small = [
         pltpu.make_async_copy(flips_hbm, flips_ref, small_sem.at[0]),
         pltpu.make_async_copy(picks_hbm, picks_ref, small_sem.at[1]),
-        pltpu.make_async_copy(picks_hbm.at[me // 2], mine_sm, small_sem.at[2]),
+        pltpu.make_async_copy(picks_hbm.at[me >> 1], mine_sm, small_sem.at[2]),
     ]
-    for copy in small:
-        copy.start()
+    small[0].start()
     loads = []
     for i in range(LOADS):
         rows = pl.ds(i * (ROWS // LOADS), ROWS // LOADS)
         loads.append(pltpu.make_async_copy(panel_ref.at[rows], x_ref.at[rows], load_sem.at[i]))
         loads[-1].start()
-
+    small[1].start()
+    small[2].start()
     barrier = pltpu.get_barrier_semaphore()
+    for _, spot in here.others():
+        pl.semaphore_signal(barrier, inc=1, device_id=spot, device_id_type=MESH)
+
     small[0].wait()
     signs = (1 - 2 * flips_ref[...]).astype(jnp.float32).T
     for g in range(32):
-        for k in range(4 * g, 4 * g + 4):
-            if k > 0:
-                pl.semaphore_signal(
-                    barrier, inc=1, device_id=place(partner(me, k)), device_id_type=MESH
-                )
         if g % (32 // LOADS) == 0:
             loads[g // (32 // LOADS)].wait()
         first_pass(x_ref, signs, t_ref, g)
@@ -159,28 +182,27 @@
     def rows_of(d, half):
         return pl.ds(pl.multiple_of(d * CHUNK + half * HALF, HALF), HALF)
 
+    def send(src, dst, send_sem, recv_sem, spot):
+        pltpu.make_async_remote_copy(
+            src, dst, send_sem, recv_sem, device_id=spot, device_id_type=MESH
+        ).start()
+
     def send_in(half):
-        def one(d):
-            pltpu.make_async_remote_copy(
-                t_ref.at[rows_of(d, half)], in_ref.at[me, pl.ds(half * HALF, HALF)],
-                p1s.at[half], p1r.at[half], device_id=place(d), device_id_type=MESH,
-            ).start()
-
-        each_partner(me, one)
+        part = pl.ds(half * HALF, HALF)
+        for d, spot in here.others():
+            send(t_ref.at[rows_of(d, half)], in_ref.at[me, part], p1s.at[half], p1r.at[half], spot)
 
     def send_back(half):
-        def one(d):
-            pltpu.make_async_remote_copy(
-                done_ref.at[d, pl.ds(half * HALF, HALF)], mixed_ref.at[rows_of(me, half)],
-                p2s.at[half], p2r.at[half], device_id=place(d), device_id_type=MESH,
-            ).start()
-
-        each_partner(me, one)
-
-    others = pl.ds(0, (DEV - 1) * HALF)
+        part = pl.ds(half * HALF, HALF)
+        for d, spot in here.others():
+            send(done_ref.at[d, part], mixed_ref.at[rows_of(me, half)], p2s.at[half], p2r.at[half], spot)
 
     def wait_bytes(sem):
+        others = pl.ds(0, (DEV - 1) * HALF)
         pltpu.make_async_copy(x_ref.at[others], t_ref.at[others], sem).wait()
+
+    def wait_rows(ref, sem):
+        pltpu.make_async_copy(ref.at[pl.ds(0, DEV - 1)], ref.at[pl.ds(0, DEV - 1)], sem).wait()
 
     def add_gram(half):
         def step(g, total):
@@ -215,55 +237,44 @@
     add_gram(0)
     wait_bytes(p1r.at[1])
     device_transform(1, in_ref, done_ref)
+    add_gram(1)
+    gp_out[...] = part_ref[...].reshape(DEV, 1, COLS)
+    for d, spot in here.others():
+        send(gp_out.at[d], gp_in.at[me], gps, gpr, spot)
     send_back(1)
+    gp_in[me] = gp_out[me]
     mixed_ref[pl.ds(pl.multiple_of(me * CHUNK, CHUNK), CHUNK), :] = done_ref[me]
-    add_gram(1)
-    gp_out[...] = part_ref[...].reshape(COLS, 1, COLS)
-
-    def send(src, dst, send_sem, recv_sem, d):
-        pltpu.make_async_remote_copy(
-            src, dst, send_sem, recv_sem, device_id=place(d), device_id_type=MESH
-        ).start()
-
-    def wait_rows(ref, sem):
-        pltpu.make_async_copy(ref.at[pl.ds(0, DEV - 1)], ref.at[pl.ds(0, DEV - 1)], sem).wait()
-
-    each_partner(me, lambda d: send(gp_out.at[d], gp_in.at[me], gps, gpr, d))
-    gp_in[me] = gp_out[me]
     wait_rows(gp_in, gpr)
     gram_row = jnp.sum(gp_in[...], axis=0, keepdims=True) * (1.0 / 8192.0)
-    row_out[:, 1:2, :] = jnp.broadcast_to(gram_row, (DEV, 1, COLS))
-
+    row_out[:, 1] = jnp.broadcast_to(gram_row, (DEV, 1, COLS))
+
+    wanted.wait()
     wait_bytes(p2r.at[0])
     wait_bytes(p2r.at[1])
-    wanted.wait()
-
-    def row_for(d):
-        row_out[d, 0:1, :] = mixed_ref[pl.ds(wanted_sm[d // 2, d % 2], 1), :]
-
-    def send_row(d):
-        row_for(d)
-        send(row_out.at[d], row_in.at[me], rows_s, rows_r, d)
-
-    each_partner(me, send_row)
-    row_for(me)
+
+    def gather(k, carry):
+        for j in range(2):
+            row_out[2 * k + j, 0] = mixed_ref[pl.ds(wanted_sm[k, j], 1), :]
+        return carry
+
+    lax.fori_loop(0, DEV // 2, gather, 0, unroll=8)
+    for d, spot in here.others():
+        send(row_out.at[d], row_in.at[me], rows_s, rows_r, spot)
     row_in[me] = row_out[me]
-
     small[2].wait()
-    wait_rows(row_in, rows_r)
-    gram_ref[...] = row_in[:, 1, :]
-    start = (me % 2) * 64
-
-    def pick_row(i, carry):
-        owner = (mine_sm[start + i] >> 12) & (DEV - 1)
-        sketch_ref[pl.ds(i, 1), :] = row_in[owner, 0:1, :]
-        return carry
-
-    lax.fori_loop(0, 64, pick_row, 0, unroll=8)
     for half in range(2):
         wait_bytes(p1s.at[half])
         wait_bytes(p2s.at[half])
     wait_rows(gp_in, gps)
+    wait_rows(row_in, rows_r)
+    start = (me & 1) * 64
+
+    def pick_row(i, carry):
+        sketch_ref[pl.ds(i, 1), :] = row_in[(mine_sm[start + i] >> 12) & (DEV - 1), 0]
+        return carry
+
+    lax.fori_loop(0, 64, pick_row, 0, unroll=16)
+    gram_ref[...] = row_in[:, 1].reshape(COLS, COLS)
     wait_rows(row_in, rows_s)
 
 
@@ -299,8 +310,8 @@
             pltpu.VMEM((64, 128), i32),
             pltpu.SMEM((64, 128), i32),
             pltpu.SMEM((128,), i32),
-            pltpu.VMEM((DEV, 2, COLS), f32),
-            pltpu.VMEM((DEV, 2, COLS), f32),
+            pltpu.VMEM((DEV, 2, 1, COLS), f32),
+            pltpu.VMEM((DEV, 2, 1, COLS), f32),
             pltpu.VMEM((DEV, 1, COLS), f32),
             pltpu.VMEM((DEV, 1, COLS), f32),
             dma((LOADS,)), dma((3,)), dma((2,)), dma((2,)), dma((2,)), dma((2,)),
@@ -318,7 +329,7 @@
         out_specs=(hbm, hbm, hbm),
         scratch_shapes=[dma((3,))],
         name="leave",
-    )(*parts)
+    )(*(pltpu.with_memory_space_constraint(p, pltpu.VMEM) for p in parts))
 
 
 def solution(mesh):

time: 80.9 us -> 67.6 us (0.84)
  Pallas kernels: 77.5 us -> 66.8 us
  local copies, waits for them, and re-layouts: 2.54 us -> 0 us
    pallas_call x1, Pallas kernels: 74.6 us -> 65.5 us  [on_device(): pl.pallas_call(kernel, out_shape=tuple((pltpu.VMEM(shape, f32) for shape...]
    unnamed x6 -> x0, local copies, waits for them, and re-layouts: 2.54 us -> none
    pallas_call x1, Pallas kernels: 2.97 us -> 1.36 us  [on_device(): pl.pallas_call(leave_kernel, out_shape=tuple((jax.ShapeDtypeStruct(shape,...]
where the time goes in v3:
time: 67.6 us; the launch traced here: 67.5 us
  Pallas kernels  66.8 us (99%)
    pallas_call x1, Pallas kernels, on_device(): pl.pallas_call(kernel, out_shape=tuple((pltpu.VMEM(shape, f32) for shape...  65.5 us
    pallas_call x1, Pallas kernels, on_device(): pl.pallas_call(leave_kernel, out_shape=tuple((jax.ShapeDtypeStruct(shape,...  1.36 us

profile of v3, /device:TPU:1, one launch (start us, length us, event | category | flops | bytes accessed | tf_op | source)
XLA Modules:
  0.0 67.5 jit_solution(9561611037736857090)
XLA Ops:
  0.6 65.5 %sketch.1 = (f32[4096,128]{1,0:T(8,128)S(1)}, f32[64,128]{1,0:T(8,128)S(1)}, f32[128,128]{1,0:T(8,128)S(1)}) custom-call(f32[4096,128]{1,0:T(8,128)} %panel_ref.1, s32[32,128]{1,0:T(8,128)} %bitcast.3, s32[64,128]{1,0:T(8,128)} %bitcast.2), custom_call_target="tpu_custom_call" | custom-call | tf_op jit(solution)/shard_map/sketch/pallas_call | solution.py:296
  66.1 1.4 %leave.1 = (f32[4096,128]{1,0:T(8,128)}, f32[64,128]{1,0:T(8,128)}, f32[128,128]{1,0:T(8,128)}) custom-call(f32[4096,128]{1,0:T(8,128)S(1)} %get-tuple-element.6.mixed_ref, f32[64,128]{1,0:T(8,128)S(1)} %get-tuple-element.7.sketch_ref, f32[128,128]{1,0:T(8,128)S(1)} %get-tuple-element.8.gram_ref), custom_call_target="tpu_custom_call" | custom-call | tf_op jit(solution)/shard_map/leave/pallas_call | solution.py:325

commit v4 on v3

--- a/solution.py
+++ b/solution.py
@@ -42,6 +42,9 @@
 
 
 OFFSETS = offsets()
+FAR_FIRST = OFFSETS
+CROSS = [o for o in OFFSETS if o[3] == 1 and sum(min(v, 4 - v) for v in o[:3]) == 1]
+OFFSETS = CROSS + [o for o in OFFSETS if o not in CROSS]
 
 
 class Place:
@@ -56,8 +59,8 @@
         self.zn = [(((z + i) >> 1) & 1) * 2 for i in range(4)]
         self.cs = [core, 1 - core]
 
-    def others(self):
-        for dx, dy, dz, dc in OFFSETS:
+    def others(self, offsets=OFFSETS):
+        for dx, dy, dz, dc in offsets:
             narrow, wide = self.zn[dz] + self.cs[dc], self.xs[dx] + self.ys[dy] + self.zs[dz]
             yield narrow * 32 + wide, (narrow, wide)
 
@@ -90,7 +93,7 @@
             t_ref[pl.ds(s, 8, stride=8), :] = value
         return carry
 
-    lax.fori_loop(0, 32, step, 0, unroll=4)
+    lax.fori_loop(0, 32, step, 0, unroll=8)
 
 
 def third_pass(half, t_ref):
@@ -102,7 +105,7 @@
             t_ref[pl.ds(s, 8), :] = value
         return carry
 
-    lax.fori_loop(0, 16, step, 0, unroll=4)
+    lax.fori_loop(0, 16, step, 0, unroll=8)
 
 
 def device_transform(half, src_ref, dst_ref):
@@ -152,6 +155,9 @@
 ):
     here = Place()
     me = here.me
+    barrier = pltpu.get_barrier_semaphore()
+    for _, spot in here.others(FAR_FIRST):
+        pl.semaphore_signal(barrier, inc=1, device_id=spot, device_id_type=MESH)
     small = [
         pltpu.make_async_copy(flips_hbm, flips_ref, small_sem.at[0]),
         pltpu.make_async_copy(picks_hbm, picks_ref, small_sem.at[1]),
@@ -165,10 +171,6 @@
         loads[-1].start()
     small[1].start()
     small[2].start()
-    barrier = pltpu.get_barrier_semaphore()
-    for _, spot in here.others():
-        pl.semaphore_signal(barrier, inc=1, device_id=spot, device_id_type=MESH)
-
     small[0].wait()
     signs = (1 - 2 * flips_ref[...]).astype(jnp.float32).T
     for g in range(32):
@@ -212,7 +214,7 @@
                 left, rows, precision=lax.Precision.HIGHEST, preferred_element_type=jnp.float32
             )
 
-        part_ref[...] = lax.fori_loop(0, 16, step, part_ref[...])
+        part_ref[...] = lax.fori_loop(0, 16, step, part_ref[...], unroll=4)
 
     send_in(0)
     third_pass(1, t_ref)

time: 67.6 us -> 67.1 us (level)
  no operation moved by 1% of the time
where the time goes in v4:
time: 67.1 us; the launch traced here: 67 us
  Pallas kernels  66.3 us (99%)
    pallas_call x1, Pallas kernels, on_device(): pl.pallas_call(kernel, out_shape=tuple((pltpu.VMEM(shape, f32) for shape...  65 us
    pallas_call x1, Pallas kernels, on_device(): pl.pallas_call(leave_kernel, out_shape=tuple((jax.ShapeDtypeStruct(shape,...  1.36 us

profile of v4, /device:TPU:1, one launch (start us, length us, event | category | flops | bytes accessed | tf_op | source)
XLA Modules:
  0.0 67.0 jit_solution(15240262160287529205)
XLA Ops:
  0.6 65.0 %sketch.1 = (f32[4096,128]{1,0:T(8,128)S(1)}, f32[64,128]{1,0:T(8,128)S(1)}, f32[128,128]{1,0:T(8,128)S(1)}) custom-call(f32[4096,128]{1,0:T(8,128)} %panel_ref.1, s32[32,128]{1,0:T(8,128)} %bitcast.3, s32[64,128]{1,0:T(8,128)} %bitcast.2), custom_call_target="tpu_custom_call" | custom-call | tf_op jit(solution)/shard_map/sketch/pallas_call | solution.py:298
  65.6 1.4 %leave.1 = (f32[4096,128]{1,0:T(8,128)}, f32[64,128]{1,0:T(8,128)}, f32[128,128]{1,0:T(8,128)}) custom-call(f32[4096,128]{1,0:T(8,128)S(1)} %get-tuple-element.6.mixed_ref, f32[64,128]{1,0:T(8,128)S(1)} %get-tuple-element.7.sketch_ref, f32[128,128]{1,0:T(8,128)S(1)} %get-tuple-element.8.gram_ref), custom_call_target="tpu_custom_call" | custom-call | tf_op jit(solution)/shard_map/leave/pallas_call | solution.py:327

commit v5 on v4

--- a/solution.py
+++ b/solution.py
@@ -45,6 +45,9 @@
 FAR_FIRST = OFFSETS
 CROSS = [o for o in OFFSETS if o[3] == 1 and sum(min(v, 4 - v) for v in o[:3]) == 1]
 OFFSETS = CROSS + [o for o in OFFSETS if o not in CROSS]
+NEAR = [o for o in FAR_FIRST if 1 <= sum(min(v, 4 - v) for v in o[:3]) <= 3]
+DIRECT = [o for o in FAR_FIRST if o not in NEAR or o[3] == 0]
+PASSED_ON = [o for o in NEAR if o[3] == 0]
 
 
 class Place:
@@ -58,6 +61,7 @@
         self.zs = [((z + i) & 1) * 4 for i in range(4)]
         self.zn = [(((z + i) >> 1) & 1) * 2 for i in range(4)]
         self.cs = [core, 1 - core]
+        self.core, self.twin = core, (self.narrow ^ 1, self.wide)
 
     def others(self, offsets=OFFSETS):
         for dx, dy, dz, dc in offsets:
@@ -150,8 +154,8 @@
     panel_ref, flips_hbm, picks_hbm,
     mixed_ref, sketch_ref, gram_ref,
     x_ref, t_ref, in_ref, done_ref, flips_ref, picks_ref, counts_ref, part_ref, wanted_ref, wanted_sm, mine_sm,
-    row_out, row_in, gp_out, gp_in,
-    load_sem, small_sem, p1s, p1r, p2s, p2r, gps, gpr, rows_s, rows_r,
+    row_out, row_in, passed, gp_out, gp_in,
+    load_sem, small_sem, p1s, p1r, p2s, p2r, gps, gpr, rows_s, rows_r, fws, fwr,
 ):
     here = Place()
     me = here.me
@@ -260,8 +264,22 @@
         return carry
 
     lax.fori_loop(0, DEV // 2, gather, 0, unroll=8)
-    for d, spot in here.others():
+    swaps = []
+    for side in range(2):
+        block = pl.ds(pl.multiple_of(side * 64 + (1 - here.core) * 32, 32), 32)
+        swaps.append(
+            pltpu.make_async_remote_copy(
+                row_out.at[block], passed.at[side], fws.at[side], fwr.at[side],
+                device_id=here.twin, device_id_type=MESH,
+            )
+        )
+        swaps[-1].start()
+    for d, spot in here.others(DIRECT):
         send(row_out.at[d], row_in.at[me], rows_s, rows_r, spot)
+    for swap in swaps:
+        swap.wait()
+    for _, (narrow, wide) in here.others(PASSED_ON):
+        send(passed.at[narrow >> 1, wide], row_in.at[me ^ 32], rows_s, rows_r, (narrow, wide))
     row_in[me] = row_out[me]
     small[2].wait()
     for half in range(2):
@@ -314,10 +332,11 @@
             pltpu.SMEM((128,), i32),
             pltpu.VMEM((DEV, 2, 1, COLS), f32),
             pltpu.VMEM((DEV, 2, 1, COLS), f32),
+            pltpu.VMEM((2, 32, 2, 1, COLS), f32),
             pltpu.VMEM((DEV, 1, COLS), f32),
             pltpu.VMEM((DEV, 1, COLS), f32),
             dma((LOADS,)), dma((3,)), dma((2,)), dma((2,)), dma((2,)), dma((2,)),
-            dma, dma, dma, dma,
+            dma, dma, dma, dma, dma((2,)), dma((2,)),
         ],
         name="sketch",
         compiler_params=pltpu.CompilerParams(

time: 67.1 us -> 67.1 us (level)
  no operation moved by 1% of the time
where the time goes in v5:
time: 67.1 us; the launch traced here: 67 us
  Pallas kernels  66.3 us (99%)
    pallas_call x1, Pallas kernels, on_device(): pl.pallas_call(kernel, out_shape=tuple((pltpu.VMEM(shape, f32) for shape...  65 us
    pallas_call x1, Pallas kernels, on_device(): pl.pallas_call(leave_kernel, out_shape=tuple((jax.ShapeDtypeStruct(shape,...  1.36 us

profile of v5, /device:TPU:1, one launch (start us, length us, event | category | flops | bytes accessed | tf_op | source)
XLA Modules:
  0.0 67.0 jit_solution(8962782299126272523)
XLA Ops:
  0.6 65.0 %sketch.1 = (f32[4096,128]{1,0:T(8,128)S(1)}, f32[64,128]{1,0:T(8,128)S(1)}, f32[128,128]{1,0:T(8,128)S(1)}) custom-call(f32[4096,128]{1,0:T(8,128)} %panel_ref.1, s32[32,128]{1,0:T(8,128)} %bitcast.3, s32[64,128]{1,0:T(8,128)} %bitcast.2), custom_call_target="tpu_custom_call" | custom-call | tf_op jit(solution)/shard_map/sketch/pallas_call | solution.py:316
  65.6 1.4 %leave.1 = (f32[4096,128]{1,0:T(8,128)}, f32[64,128]{1,0:T(8,128)}, f32[128,128]{1,0:T(8,128)}) custom-call(f32[4096,128]{1,0:T(8,128)S(1)} %get-tuple-element.6.mixed_ref, f32[64,128]{1,0:T(8,128)S(1)} %get-tuple-element.7.sketch_ref, f32[128,128]{1,0:T(8,128)S(1)} %get-tuple-element.8.gram_ref), custom_call_target="tpu_custom_call" | custom-call | tf_op jit(solution)/shard_map/leave/pallas_call | solution.py:346

commit v6 on v4

--- a/solution.py
+++ b/solution.py
@@ -45,6 +45,7 @@
 FAR_FIRST = OFFSETS
 CROSS = [o for o in OFFSETS if o[3] == 1 and sum(min(v, 4 - v) for v in o[:3]) == 1]
 OFFSETS = CROSS + [o for o in OFFSETS if o not in CROSS]
+SAME_CORE = [o for o in OFFSETS if o[3] == 0]
 
 
 class Place:
@@ -58,6 +59,7 @@
         self.zs = [((z + i) & 1) * 4 for i in range(4)]
         self.zn = [(((z + i) >> 1) & 1) * 2 for i in range(4)]
         self.cs = [core, 1 - core]
+        self.side = self.narrow >> 1
 
     def others(self, offsets=OFFSETS):
         for dx, dy, dz, dc in offsets:
@@ -206,6 +208,10 @@
     def wait_rows(ref, sem):
         pltpu.make_async_copy(ref.at[pl.ds(0, DEV - 1)], ref.at[pl.ds(0, DEV - 1)], sem).wait()
 
+    def wait_sums(sem):
+        rows = row_in.at[pl.ds(0, 42)]
+        pltpu.make_async_copy(rows, rows, sem).wait()
+
     def add_gram(half):
         def step(g, total):
             rows = done_ref[pl.ds(g * 8, 8), pl.ds(half * HALF, HALF), :].reshape(128, COLS)
@@ -240,15 +246,19 @@
     wait_bytes(p1r.at[1])
     device_transform(1, in_ref, done_ref)
     add_gram(1)
-    gp_out[...] = part_ref[...].reshape(DEV, 1, COLS)
-    for d, spot in here.others():
-        send(gp_out.at[d], gp_in.at[me], gps, gpr, spot)
+    for core in range(2):
+        for side in range(2):
+            rows = pl.ds((2 * side + core) * 32, 32)
+            gp_out[side, :, core] = part_ref[rows, :].reshape(32, 1, COLS)
+    for _, (narrow, wide) in here.others(SAME_CORE):
+        send(gp_out.at[narrow >> 1, wide], gp_in.at[here.side, here.wide], gps, gpr, (narrow, wide))
     send_back(1)
-    gp_in[me] = gp_out[me]
+    gp_in[here.side, here.wide] = gp_out[here.side, here.wide]
     mixed_ref[pl.ds(pl.multiple_of(me * CHUNK, CHUNK), CHUNK), :] = done_ref[me]
-    wait_rows(gp_in, gpr)
-    gram_row = jnp.sum(gp_in[...], axis=0, keepdims=True) * (1.0 / 8192.0)
-    row_out[:, 1] = jnp.broadcast_to(gram_row, (DEV, 1, COLS))
+    wait_sums(gpr)
+    sums = jnp.sum(gp_in[...], axis=(0, 1)) * (1.0 / 8192.0)
+    for core in range(2):
+        row_out[:, 1 + core] = jnp.broadcast_to(sums[core : core + 1], (DEV, 1, COLS))
 
     wanted.wait()
     wait_bytes(p2r.at[0])
@@ -267,7 +277,7 @@
     for half in range(2):
         wait_bytes(p1s.at[half])
         wait_bytes(p2s.at[half])
-    wait_rows(gp_in, gps)
+    wait_sums(gps)
     wait_rows(row_in, rows_r)
     start = (me & 1) * 64
 
@@ -276,7 +286,10 @@
         return carry
 
     lax.fori_loop(0, 64, pick_row, 0, unroll=16)
-    gram_ref[...] = row_in[:, 1].reshape(COLS, COLS)
+    for side in range(2):
+        for core in range(2):
+            first, second = (row_in[pl.ds(side * 64 + 32 * c, 32), 1 + core] for c in range(2))
+            gram_ref[pl.ds(side * 64 + 32 * core, 32), :] = (first + second).reshape(32, COLS)
     wait_rows(row_in, rows_s)
 
 
@@ -312,10 +325,10 @@
             pltpu.VMEM((64, 128), i32),
             pltpu.SMEM((64, 128), i32),
             pltpu.SMEM((128,), i32),
-            pltpu.VMEM((DEV, 2, 1, COLS), f32),
-            pltpu.VMEM((DEV, 2, 1, COLS), f32),
-            pltpu.VMEM((DEV, 1, COLS), f32),
-            pltpu.VMEM((DEV, 1, COLS), f32),
+            pltpu.VMEM((DEV, 3, 1, COLS), f32),
+            pltpu.VMEM((DEV, 3, 1, COLS), f32),
+            pltpu.VMEM((2, 32, 2, 1, COLS), f32),
+            pltpu.VMEM((2, 32, 2, 1, COLS), f32),
             dma((LOADS,)), dma((3,)), dma((2,)), dma((2,)), dma((2,)), dma((2,)),
             dma, dma, dma, dma,
         ],

time: 67.1 us -> 67.5 us (level)
  no operation moved by 1% of the time
where the time goes in v6:
time: 67.5 us; the launch traced here: 67.4 us
  Pallas kernels  66.8 us (99%)
    pallas_call x1, Pallas kernels, on_device(): pl.pallas_call(kernel, out_shape=tuple((pltpu.VMEM(shape, f32) for shape...  65.4 us
    pallas_call x1, Pallas kernels, on_device(): pl.pallas_call(leave_kernel, out_shape=tuple((jax.ShapeDtypeStruct(shape,...  1.36 us

profile of v6, /device:TPU:1, one launch (start us, length us, event | category | flops | bytes accessed | tf_op | source)
XLA Modules:
  0.0 67.4 jit_solution(3808439609757071497)
XLA Ops:
  0.6 65.4 %sketch.1 = (f32[4096,128]{1,0:T(8,128)S(1)}, f32[64,128]{1,0:T(8,128)S(1)}, f32[128,128]{1,0:T(8,128)S(1)}) custom-call(f32[4096,128]{1,0:T(8,128)} %panel_ref.1, s32[32,128]{1,0:T(8,128)} %bitcast.3, s32[64,128]{1,0:T(8,128)} %bitcast.2), custom_call_target="tpu_custom_call" | custom-call | tf_op jit(solution)/shard_map/sketch/pallas_call | solution.py:311
  66.0 1.4 %leave.1 = (f32[4096,128]{1,0:T(8,128)}, f32[64,128]{1,0:T(8,128)}, f32[128,128]{1,0:T(8,128)}) custom-call(f32[4096,128]{1,0:T(8,128)S(1)} %get-tuple-element.6.mixed_ref, f32[64,128]{1,0:T(8,128)S(1)} %get-tuple-element.7.sketch_ref, f32[128,128]{1,0:T(8,128)S(1)} %get-tuple-element.8.gram_ref), custom_call_target="tpu_custom_call" | custom-call | tf_op jit(solution)/shard_map/leave/pallas_call | solution.py:340

commit v7 on v4

--- a/solution.py
+++ b/solution.py
@@ -281,10 +281,11 @@
 
 
 def leave_kernel(mixed_ref, sketch_ref, gram_ref, mixed_out, sketch_out, gram_out, sems):
-    pairs = ((mixed_ref, mixed_out), (sketch_ref, sketch_out), (gram_ref, gram_out))
+    n = ROWS // 2
+    pairs = tuple((mixed_ref.at[pl.ds(i * n, n)], mixed_out.at[pl.ds(i * n, n)]) for i in range(2)) + ((sketch_ref, sketch_out), (gram_ref, gram_out))
     copies = [pltpu.make_async_copy(a, b, sems.at[i]) for i, (a, b) in enumerate(pairs)]
-    for copy in copies:
-        copy.start()
+    for i, copy in enumerate(copies):
+        copy.start(priority=i % 2)
     for copy in copies:
         copy.wait()
 
@@ -329,7 +330,7 @@
         out_shape=tuple(jax.ShapeDtypeStruct(shape, f32) for shape in shapes),
         in_specs=[vmem, vmem, vmem],
         out_specs=(hbm, hbm, hbm),
-        scratch_shapes=[dma((3,))],
+        scratch_shapes=[dma((4,))],
         name="leave",
     )(*(pltpu.with_memory_space_constraint(p, pltpu.VMEM) for p in parts))
 

time: 67.1 us -> 67.1 us (level)
  no operation moved by 1% of the time
where the time goes in v7:
time: 67.1 us; the launch traced here: 67 us
  Pallas kernels  66.3 us (99%)
    pallas_call x1, Pallas kernels, on_device(): pl.pallas_call(kernel, out_shape=tuple((pltpu.VMEM(shape, f32) for shape...  65 us
    pallas_call x1, Pallas kernels, on_device(): pl.pallas_call(leave_kernel, out_shape=tuple((jax.ShapeDtypeStruct(shape,...  1.37 us

profile of v7, /device:TPU:1, one launch (start us, length us, event | category | flops | bytes accessed | tf_op | source)
XLA Modules:
  0.0 67.0 jit_solution(16178546366337009786)
XLA Ops:
  0.6 65.0 %sketch.1 = (f32[4096,128]{1,0:T(8,128)S(1)}, f32[64,128]{1,0:T(8,128)S(1)}, f32[128,128]{1,0:T(8,128)S(1)}) custom-call(f32[4096,128]{1,0:T(8,128)} %panel_ref.1, s32[32,128]{1,0:T(8,128)} %bitcast.3, s32[64,128]{1,0:T(8,128)} %bitcast.2), custom_call_target="tpu_custom_call" | custom-call | tf_op jit(solution)/shard_map/sketch/pallas_call | solution.py:299
  65.6 1.4 %leave.1 = (f32[4096,128]{1,0:T(8,128)}, f32[64,128]{1,0:T(8,128)}, f32[128,128]{1,0:T(8,128)}) custom-call(f32[4096,128]{1,0:T(8,128)S(1)} %get-tuple-element.6.mixed_ref, f32[64,128]{1,0:T(8,128)S(1)} %get-tuple-element.7.sketch_ref, f32[128,128]{1,0:T(8,128)S(1)} %get-tuple-element.8.gram_ref), custom_call_target="tpu_custom_call" | custom-call | tf_op jit(solution)/shard_map/leave/pallas_call | solution.py:328
